TPU v7x, 32 devices: a whole 2x2x4 slice. The times are simulated.
32 devices in a mesh: row: 8 (over y, x, core), col: 4 (over z).
Axes of the slice: x: 2, y: 2, z: 4, core: 2. Of those that a mesh axis runs over, the one named last changes fastest.
Arguments:
- tokens: bfloat16 [512, 12288], P('row', 'col'), may hold values from -6 to 6
- out_grad: bfloat16 [512, 12288], P('row', 'col'), may hold values from -6 to 6
- w_in: bfloat16 [12288, 24576], P('col', 'row'), may hold values from -0.0546875 to 0.0546875
- w_out: bfloat16 [24576, 12288], P('row', 'col'), may hold values from -0.0390625 to 0.0390625
- bias_in: float32 [24576], P('row'), may hold values from -3 to 3
- stream_ids: int32 [3], replicated, may hold values from 0 to 4095
- tile_keys: int32 [64, 192], replicated, may hold values from 0 to 16777215
Outputs:
- grad_tokens: bfloat16 [512, 12288], P('row', 'col')
- grad_w_in: bfloat16 [12288, 24576], P('col', 'row')
- grad_w_out: bfloat16 [24576, 12288], P('row', 'col')
- grad_bias_in: float32 [24576], P('row')
- grad_bias_out: float32 [12288], P('col')
All inputs are finite; a program needn't handle non-finite values.
Results may differ from a plain program's by a relative error of at most 0.005.
Values may be sent and summed in bfloat16 or wider, within the bound.
A program may use at most 192 MiB of HBM per device.

v0:
```python
import jax
import jax.numpy as jnp
from jax import lax
from jax.sharding import PartitionSpec as P

TILE_T = 8
TILE_F = 128


mix_one = 73856093
mix_two = 19349663
mix_three = 83492791
golden = -1640531535
mult_one = 2146121005
mult_two = -2073254261


def shift_down(value, count):
    return lax.shift_right_logical(value, jnp.full(value.shape, count, jnp.int32))


def keep_mask(tile_keys, stream_ids, row_count, col_start, col_count, tile_t, tile_f):
    row_ids = jnp.arange(row_count, dtype=jnp.int32)
    col_ids = col_start + jnp.arange(col_count, dtype=jnp.int32)
    onehot_rows = (
        row_ids[:, None] // tile_t == jnp.arange(tile_keys.shape[0], dtype=jnp.int32)[None, :]
    ).astype(jnp.int32)
    onehot_cols = (
        jnp.arange(tile_keys.shape[1], dtype=jnp.int32)[:, None] == col_ids[None, :] // tile_f
    ).astype(jnp.int32)
    picked = jnp.dot(onehot_rows, tile_keys, preferred_element_type=jnp.int32)
    picked = jnp.dot(picked, onehot_cols, preferred_element_type=jnp.int32)
    salt = (
        stream_ids[0] * jnp.int32(mix_one)
        ^ stream_ids[1] * jnp.int32(mix_two)
        ^ stream_ids[2] * jnp.int32(mix_three)
    )
    offset = row_ids[:, None] % tile_t * tile_f + col_ids[None, :] % tile_f
    value = (picked ^ salt) + offset * jnp.int32(golden)
    value = value ^ shift_down(value, 16)
    value = value * jnp.int32(mult_one)
    value = value ^ shift_down(value, 15)
    value = value * jnp.int32(mult_two)
    value = value ^ shift_down(value, 16)
    return (shift_down(value, 8) & jnp.int32(1023) < jnp.int32(922)).astype(jnp.float32)


def normal_cdf(value):
    return 0.5 * (1.0 + lax.erf(value * 0.7071067811865476))


def local_gelu(pre_part, dact_part, bias_part, keep):
    pre = pre_part + bias_part
    scaled = keep * (1.0 / 0.9)
    cdf = normal_cdf(pre)
    act = (pre * cdf * scaled).astype(jnp.bfloat16)
    slope = cdf + pre * jnp.exp(-0.5 * pre * pre) * 0.3989422804014327
    dpre = (dact_part * scaled * slope).astype(jnp.bfloat16)
    return (act, dpre)


def local(tokens, out_grad, w_in, w_out, bias_in, stream_ids, tile_keys):
    col_count = lax.axis_size("col")
    row_index = lax.axis_index("row")
    col_index = lax.axis_index("col")
    ff_local = w_in.shape[1]
    all_tokens, all_grads = (
        lax.all_gather(tokens, "row", axis=0, tiled=True),
        lax.all_gather(out_grad, "row", axis=0, tiled=True),
    )
    total_tokens = all_tokens.shape[0]
    pre_terms = jnp.dot(all_tokens, w_in, preferred_element_type=jnp.float32)
    dact_terms = lax.dot_general(
        all_grads, w_out, (((1,), (1,)), ((), ())), preferred_element_type=jnp.float32
    )
    pre_part, dact_part = (
        lax.psum_scatter(pre_terms, "col", scatter_dimension=1, tiled=True),
        lax.psum_scatter(dact_terms, "col", scatter_dimension=1, tiled=True),
    )
    width = ff_local // col_count
    col_start = row_index * ff_local + col_index * width
    bias_part = lax.dynamic_slice_in_dim(bias_in, col_index * width, width, 0)
    keep = keep_mask(tile_keys, stream_ids, total_tokens, col_start, width, TILE_T, TILE_F)
    act, dpre = local_gelu(pre_part, dact_part, bias_part[None, :], keep)
    act_all, dpre_all = (
        lax.all_gather(act, "col", axis=1, tiled=True),
        lax.all_gather(dpre, "col", axis=1, tiled=True),
    )
    grad_w_out = lax.dot_general(
        act_all, all_grads, (((0,), (0,)), ((), ())), preferred_element_type=jnp.float32
    ).astype(jnp.bfloat16)
    grad_w_in = lax.dot_general(
        all_tokens, dpre_all, (((0,), (0,)), ((), ())), preferred_element_type=jnp.float32
    ).astype(jnp.bfloat16)
    grad_tokens = lax.psum_scatter(
        lax.dot_general(
            dpre_all, w_in, (((1,), (1,)), ((), ())), preferred_element_type=jnp.float32
        ),
        "row",
        scatter_dimension=0,
        tiled=True,
    ).astype(jnp.bfloat16)
    grad_bias_in = jnp.sum(dpre_all.astype(jnp.float32), axis=0)
    grad_bias_out = jnp.sum(all_grads.astype(jnp.float32), axis=0)
    return (grad_tokens, grad_w_in, grad_w_out, grad_bias_in, grad_bias_out)


def solution(mesh):
    return jax.shard_map(
        local,
        mesh=mesh,
        in_specs=(
            P("row", "col"),
            P("row", "col"),
            P("col", "row"),
            P("row", "col"),
            P("row"),
            P(),
            P(),
        ),
        out_specs=(P("row", "col"), P("col", "row"), P("row", "col"), P("row"), P("col")),
        check_vma=False,
    )
```

profile of v0, /device:TPU:0, one launch (start us, length us, event | category | flops | bytes accessed | tf_op | source)
XLA Modules:
  0.0 513.2 jit_solution(4612482146566430171)
XLA Ops:
  7.2 0.7 all-gather.5.cloned.1.call-update
  8.0 0.7 all-gather.7.cloned.1.call-update
  8.7 36.2 %all-gather.5.cloned.1.call-done = bf16[512,3072]{1,0:T(8,128)(2,1)} async-done(((bf16[64,3072]{1,0:T(8,128)(2,1)}), bf16[512,3072]{1,0:T(8,128)(2,1)}) %all-gather.5.cloned.1.call-update) | async-done | bytes 3145744 | tf_op jit(solution)/shard_map/all_gather | solution.py:69
  45.0 16.4 %fusion.31 = f32[512,3072]{1,0:T(8,128)} fusion(bf16[512,3072]{1,0:T(8,128)(2,1)} %all-gather.5.cloned.1.call-done, bf16[3072,3072]{1,0:T(8,128)(2,1)} %param.10), kind=kOutput, calls=%fused_computation.53 | convolution fusion | flops 9663676416 | bytes 28311552 | tf_op jit(solution)/shard_map/dot_general | solution.py:73
  61.4 17.8 %all-gather.7.cloned.1.call-done = bf16[512,3072]{1,0:T(8,128)(2,1)} async-done(((bf16[64,3072]{1,0:T(8,128)(2,1)}), bf16[512,3072]{1,0:T(8,128)(2,1)}) %all-gather.7.cloned.1.call-update) | async-done | bytes 3145744 | tf_op jit(solution)/shard_map/all_gather | solution.py:68
  79.2 16.3 %fusion.32 = f32[512,3072]{1,0:T(8,128)} fusion(bf16[512,3072]{1,0:T(8,128)(2,1)} %all-gather.7.cloned.1.call-done, bf16[3072,3072]{1,0:T(8,128)(2,1)} %param.9), kind=kOutput, calls=%fused_computation.54 | convolution fusion | flops 9663676416 | bytes 28311552 | tf_op jit(solution)/shard_map/dot_general | solution.py:72
  95.6 0.6 copy-done.4
  96.1 0.6 fusion.30
  98.7 0.8 dynamic_slice.3
  99.5 93.4 %reduce-scatter.4.cloned.1.call-done = f32[512,768]{1,0:T(8,128)} async-done(((f32[512,3072]{1,0:T(8,128)}), f32[512,768]{1,0:T(8,128)}) %reduce-scatter.4.cloned.1.call-update) | async-done | bytes 1572880 | tf_op jit(solution)/shard_map/reduce_scatter | solution.py:78
  192.8 114.0 %reduce-scatter.6.cloned.1.call-done = f32[512,768]{1,0:T(8,128)} async-done(((f32[512,3072]{1,0:T(8,128)}), f32[512,768]{1,0:T(8,128)}) %reduce-scatter.6.cloned.1.call-update) | async-done | bytes 1572880 | tf_op jit(solution)/shard_map/reduce_scatter | solution.py:77
  306.9 6.0 %fusion.2 = (bf16[512,768]{1,0:T(8,128)(2,1)}, bf16[512,768]{1,0:T(8,128)(2,1)}) fusion(f32[512,768]{1,0:T(8,128)} %reduce-scatter.6.cloned.1.call-done, f32[768]{0:T(1024)S(1)} %dynamic_slice.3, f32[512,768]{1,0:T(8,128)} %reduce-scatter.4.cloned.1.call-done, s32[768]{0:T(1024)S(1)} %get-tuple-element.15, s32[512]{0:T(512)S(1)} %get-tuple-element.18, ...), kind=kOutput, calls=%fused_computation.12 | convolution fusion | flops 175947776 | bytes 4781060 | tf_op jit(solution)/shard_map/dot_general | solution.py:32
  313.7 63.3 %all-gather.9.cloned.1.call-done = bf16[512,3072]{1,0:T(8,128)(2,1)} async-done(((bf16[512,768]{1,0:T(8,128)(2,1)}), bf16[512,3072]{1,0:T(8,128)(2,1)}) %all-gather.9.cloned.1.call-update) | async-done | bytes 3145744 | tf_op jit(solution)/shard_map/all_gather | solution.py:87
  377.0 16.5 %fusion.33 = f32[512,3072]{1,0:T(8,128)} fusion(bf16[512,3072]{1,0:T(8,128)(2,1)} %all-gather.9.cloned.1.call-done, bf16[3072,3072]{1,0:T(8,128)(2,1)} %param.9), kind=kOutput, calls=%fused_computation.55 | convolution fusion | flops 9663676416 | bytes 28311552 | tf_op jit(solution)/shard_map/dot_general | solution.py:96
  393.5 1.9 copy-done.2
  395.4 1.2 convert_reduce_fusion
  396.6 0.7 copy-done.3
  397.3 15.1 %convert_bitcast_fusion = bf16[3072,3072]{0,1:T(8,128)(2,1)} fusion(bf16[512,3072]{1,0:T(8,128)(2,1)S(1)} %copy-done.3, bf16[512,3072]{1,0:T(8,128)(2,1)} %all-gather.7.cloned.1.call-done), kind=kOutput, calls=%fused_computation | convolution fusion | flops 9673113600 | bytes 25165824 | tf_op jit(solution)/shard_map/dot_general | solution.py:92
  412.4 24.6 %copy.12 = bf16[3072,3072]{1,0:T(8,128)(2,1)} copy(bf16[3072,3072]{0,1:T(8,128)(2,1)} %convert_bitcast_fusion) | data formatting | bytes 37748736
  437.0 3.1 convert_reduce_fusion.1
  440.1 0.5 all-gather.11.cloned.1.call-done
  440.6 15.5 %convolution_convert_fusion = bf16[3072,3072]{1,0:T(8,128)(2,1)} fusion(bf16[512,3072]{1,0:T(8,128)(2,1)} %all-gather.11.cloned.1.call-done, bf16[512,3072]{1,0:T(8,128)(2,1)S(1)} %copy-done.2), kind=kOutput, calls=%fused_computation.1 | convolution fusion | flops 9673113600 | bytes 25165824 | tf_op jit(solution)/shard_map/dot_general | solution.py:89
  456.1 48.4 %reduce-scatter.8.cloned.1.call-done = f32[64,3072]{1,0:T(8,128)} async-done(((f32[512,3072]{1,0:T(8,128)}), f32[64,3072]{1,0:T(8,128)}) %reduce-scatter.8.cloned.1.call-update) | async-done | bytes 786448 | tf_op jit(solution)/shard_map/reduce_scatter | solution.py:95
  504.5 1.9 convert_element_type.28
  (21 shorter events, 1.1 us)
Async XLA Ops:
  7.2 299.7 %copy-start = (s32[64,192]{1,0:T(8,128)S(1)}, s32[64,192]{1,0:T(8,128)}, u32[]{:S(2)}) copy-start(s32[64,192]{1,0:T(8,128)} %param.13) | copy-start | bytes 147460
  7.2 37.8 %all-gather.5.cloned.1.call-start = ((), (), s32[]{:S(2)}) async-start(), calls=%async_computation.3 | async-start | bytes 3538944 | tf_op jit(solution)/shard_map/all_gather | solution.py:69
  7.9 71.3 %all-gather.7.cloned.1.call-start = ((), (), s32[]{:S(2)}) async-start(), calls=%async_computation.5 | async-start | bytes 3538944 | tf_op jit(solution)/shard_map/all_gather | solution.py:68
  8.7 184.2 %reduce-scatter.4.cloned.1.call-start = ((), (), s32[]{:S(2)}) async-start(), calls=%async_computation.4 | async-start | bytes 7864320 | tf_op jit(solution)/shard_map/reduce_scatter | solution.py:78
  61.4 245.5 %reduce-scatter.6.cloned.1.call-start = ((), (), s32[]{:S(2)}) async-start(), calls=%async_computation.6 | async-start | bytes 7864320 | tf_op jit(solution)/shard_map/reduce_scatter | solution.py:77
  95.5 0.7 copy-start.4
  95.5 281.5 %all-gather.9.cloned.1.call-start = ((), (), s32[]{:S(2)}) async-start(), calls=%async_computation.7 | async-start | bytes 3932160 | tf_op jit(solution)/shard_map/all_gather | solution.py:87
  312.9 127.7 %all-gather.11.cloned.1.call-start = ((), (), s32[]{:S(2)}) async-start(), calls=%async_computation.9 | async-start | bytes 3932160 | tf_op jit(solution)/shard_map/all_gather | solution.py:86
  313.5 191.0 %reduce-scatter.8.cloned.1.call-start = ((), (), s32[]{:S(2)}) async-start(), calls=%async_computation.8 | async-start | bytes 7077888 | tf_op jit(solution)/shard_map/reduce_scatter | solution.py:95
  393.5 1.9 copy-start.2
  395.4 1.9 copy-start.3
  440.6 65.8 %copy-start.1 = (s32[64,192]{1,0:T(8,128)S(1)}, s32[64,192]{1,0:T(8,128)}, u32[]{:S(2)}) copy-start(s32[64,192]{1,0:T(8,128)} %param.13) | copy-start | bytes 147460
Sparse Core Ops, SparseCore 0:
  9.9 35.0 all-gather.4
  46.8 32.3 all-gather.6
  82.1 110.7 reduce-scatter.3
  195.6 111.2 reduce-scatter.5
  313.0 63.9 all-gather.8
  378.4 62.1 all-gather.10
  444.0 60.4 reduce-scatter.7
where the time goes:
time: 514 us; the launch traced here: 513 us
  waiting for transfers between devices  376 us (73%)
  matrix products  85.6 us (17%)
  local copies, waits for them, and re-layouts  29.1 us (6%)
  between operations  16.1 us (3%)
  other arithmetic  6.3 us (1%)
    reduce_scatter x1, waiting for transfers between devices, local(): lax.psum_scatter(pre_terms, 'col', scatter_dimension=1, tiled=True)  114 us
    reduce_scatter x1, waiting for transfers between devices, local(): lax.psum_scatter(dact_terms, 'col', scatter_dimension=1, tiled=True)  93.4 us
    all_gather x1, waiting for transfers between devices, local(): lax.all_gather(dpre, 'col', axis=1, tiled=True)  63.3 us
    reduce_scatter x1, waiting for transfers between devices, local(): lax.psum_scatter(lax.dot_general(dpre_all, w_in, (((1,), (1,)), ((), ()))...  48.4 us
    all_gather x1, waiting for transfers between devices, local(): lax.all_gather(out_grad, 'row', axis=0, tiled=True)  36.2 us
    unnamed x11, local copies, waits for them, and re-layouts  27.7 us
    all_gather x1, waiting for transfers between devices, local(): lax.all_gather(tokens, 'row', axis=0, tiled=True)  17.8 us
    dot_general x1, matrix products, local(): lax.dot_general(dpre_all, w_in, (((1,), (1,)), ((), ())), preferred_eleme...  16.5 us
  transfers between devices with their start and end apart: 7, of which 7 were waited for; matrix products, arithmetic and copies ran while one was open for 21% of the time, Pallas kernels for 0%

commit v1 on v0

v1 whole, which is shorter than its diff:
```python
import functools

import jax
import jax.numpy as jnp
from jax import lax
from jax.experimental import pallas as pl
from jax.experimental.pallas import tpu as pltpu
from jax.sharding import PartitionSpec as P

TILE_T = 8
TILE_F = 128
MESH = pl.DeviceIdType.MESH


mix_one = 73856093
mix_two = 19349663
mix_three = 83492791
golden = -1640531535
mult_one = 2146121005
mult_two = -2073254261


def shift_down(value, count):
    return lax.shift_right_logical(value, jnp.full(value.shape, count, jnp.int32))


def keep_mask(tile_keys, stream_ids, first_tile, tile_count, per_chunk):
    salt = (
        stream_ids[0] * jnp.int32(mix_one)
        ^ stream_ids[1] * jnp.int32(mix_two)
        ^ stream_ids[2] * jnp.int32(mix_three)
    )
    token_tiles = tile_keys.shape[0]
    chunks = tile_count // per_chunk
    keys = lax.dynamic_slice_in_dim(tile_keys, first_tile, tile_count, 1) ^ salt
    keys = keys.reshape(token_tiles, chunks, per_chunk).transpose(1, 0, 2)
    shape = (chunks, token_tiles, TILE_T, per_chunk, TILE_F)
    offset = lax.broadcasted_iota(jnp.int32, shape, 2) * TILE_F + lax.broadcasted_iota(
        jnp.int32, shape, 4
    )
    value = keys[:, :, None, :, None] + offset * jnp.int32(golden)
    value = value ^ shift_down(value, 16)
    value = value * jnp.int32(mult_one)
    value = value ^ shift_down(value, 15)
    value = value * jnp.int32(mult_two)
    value = value ^ shift_down(value, 16)
    keep = (shift_down(value, 8) & jnp.int32(1023)) < jnp.int32(922)
    return keep.astype(jnp.bfloat16).reshape(chunks, token_tiles * TILE_T, per_chunk * TILE_F)


def exchange_kernel(
    n, units, slots, rows,
    tokens, grads, w_in, w_out, bias, keep,
    act, dpre, acc, bias_sum,
    own, from_left, from_right, to_right, to_left, in_ring, out_ring,
    in_sem, out_sem, right_send, right_recv, left_send, left_recv,
):
    me = lax.axis_index("col")
    right, left = lax.rem(me + 1, n), lax.rem(me + n - 1, n)
    total_rows, width = own.shape[1], own.shape[2]
    model = in_ring.shape[1]
    chunks = units // 2
    far = jnp.maximum(me, n - 1 - me)

    def fetch_in(c):
        slot = lax.rem(c, slots)
        cols = pl.ds(pl.multiple_of(c * width, width), width)
        return pltpu.make_async_copy(w_in.at[:, cols], in_ring.at[slot], in_sem.at[slot])

    def fetch_out(c):
        slot = lax.rem(c, 2)
        cols = pl.ds(pl.multiple_of(c * width, width), width)
        return pltpu.make_async_copy(w_out.at[cols, :], out_ring.at[slot], out_sem.at[slot])

    def send_right(q):
        return pltpu.make_async_remote_copy(
            src_ref=to_right.at[lax.rem(q, 2)], dst_ref=from_left.at[q],
            send_sem=right_send.at[lax.rem(q, 2)], recv_sem=right_recv.at[q],
            device_id={"col": right}, device_id_type=MESH,
        )

    def send_left(q):
        return pltpu.make_async_remote_copy(
            src_ref=to_left.at[lax.rem(q, 2)], dst_ref=from_right.at[q],
            send_sem=left_send.at[lax.rem(q, 2)], recv_sem=left_recv.at[q],
            device_id={"col": left}, device_id_type=MESH,
        )

    def own_unit(q):
        c = q // 2

        @pl.when(lax.rem(q, 2) == 0)
        def _():
            fetch_in(c).wait()

            @pl.when(c + 1 < chunks)
            def _():
                fetch_in(c + 1).start()
                fetch_out(c + 1).start()

            own[q] = jnp.dot(
                tokens[...], in_ring[lax.rem(c, slots)], preferred_element_type=jnp.float32
            )

        @pl.when(lax.rem(q, 2) == 1)
        def _():
            fetch_out(c).wait()
            own[q] = lax.dot_general(
                grads[...], out_ring[lax.rem(c, 2)], (((1,), (1,)), ((), ())),
                preferred_element_type=jnp.float32,
            )

    def pass_on(arrived, outgoing, copy, q, first, last):
        @pl.when(jnp.logical_not(first))
        def _():
            copy(q).wait_recv()

        @pl.when(jnp.logical_not(last))
        def _():
            @pl.when(q >= 2)
            def _():
                copy(q - 2).wait_send()

            @pl.when(first)
            def _():
                outgoing[lax.rem(q, 2)] = own[q].astype(outgoing.dtype)

            @pl.when(jnp.logical_not(first))
            def _():
                outgoing[lax.rem(q, 2)] = (
                    arrived[q].astype(jnp.float32) + own[q]
                ).astype(outgoing.dtype)

            copy(q).start()

    def finish(c):
        cols = pl.ds(pl.multiple_of(c * width, width), width)
        shift = bias[c]

        def add_arrived(q):
            @pl.when(me > 0)
            def _():
                own[q] += from_left[q].astype(jnp.float32)

            @pl.when(me < n - 1)
            def _():
                own[q] += from_right[q].astype(jnp.float32)

        add_arrived(2 * c)
        add_arrived(2 * c + 1)

        def block(k, total):
            at = pl.ds(pl.multiple_of(k * rows, rows), rows)
            pre = own[2 * c, at, :] + shift
            scaled = keep[c, at, :].astype(jnp.float32) * (1.0 / 0.9)
            cdf = 0.5 * (1.0 + lax.erf(pre * 0.7071067811865476))
            act[at, cols] = (pre * cdf * scaled).astype(act.dtype)
            slope = cdf + pre * jnp.exp(-0.5 * pre * pre) * 0.3989422804014327
            part = (own[2 * c + 1, at, :] * scaled * slope).astype(dpre.dtype)
            dpre[at, cols] = part
            return total + jnp.sum(part.astype(jnp.float32), axis=0, keepdims=True)

        bias_sum[c] = lax.fori_loop(
            0, total_rows // rows, block, jnp.zeros((1, width), jnp.float32)
        )
        slot = lax.rem(c, slots)

        def into(j, carry):
            at = pl.ds(pl.multiple_of(j * width, width), width)
            acc[:, at] += lax.dot_general(
                dpre[:, cols], in_ring[slot, at, :], (((1,), (1,)), ((), ())),
                preferred_element_type=jnp.float32,
            )
            return carry

        lax.fori_loop(0, model // width, into, 0)

    fetch_in(0).start()
    fetch_out(0).start()
    barrier = pltpu.get_barrier_semaphore()

    for peer in (left, right):
        pl.semaphore_signal(barrier, inc=1, device_id={"col": peer}, device_id_type=MESH)
    acc[...] = jnp.zeros_like(acc)
    own_unit(0)

    pl.semaphore_wait(barrier, 2)

    def step(s, carry):
        right_unit = s - me
        left_unit = s - (n - 1 - me)
        done = s - far

        @pl.when((right_unit >= 0) & (right_unit < units))
        def _():
            pass_on(from_left, to_right, send_right, right_unit, me == 0, me == n - 1)

        @pl.when((left_unit >= 0) & (left_unit < units))
        def _():
            pass_on(from_right, to_left, send_left, left_unit, me == n - 1, me == 0)

        @pl.when(s + 1 < units)
        def _():
            own_unit(s + 1)

        @pl.when((done >= 0) & (done < units) & (lax.rem(done + 2 * n, 2) == 1))
        def _():
            finish(done // 2)

        return carry

    lax.fori_loop(0, units + n - 1, step, 0)

    for q in (units - 2, units - 1):
        @pl.when(me < n - 1)
        def _():
            send_right(q).wait_send()

        @pl.when(me > 0)
        def _():
            send_left(q).wait_send()


def exchange(all_tokens, all_grads, w_in, w_out, bias, keep, n):
    total_rows, model = all_tokens.shape
    ff_local = w_in.shape[1]
    chunks, _, width = keep.shape
    units = 2 * chunks
    slots = n // 2 + 3
    vmem = pl.BlockSpec(memory_space=pltpu.VMEM)
    anywhere = pl.BlockSpec(memory_space=pl.ANY)
    unit_buffer = pltpu.VMEM((units, total_rows, width), jnp.bfloat16)
    unit_sems = pltpu.SemaphoreType.DMA((units,))
    return pl.pallas_call(
        functools.partial(exchange_kernel, n, units, slots, 32),
        out_shape=(
            jax.ShapeDtypeStruct((total_rows, ff_local), jnp.bfloat16),
            jax.ShapeDtypeStruct((total_rows, ff_local), jnp.bfloat16),
            jax.ShapeDtypeStruct((total_rows, model), jnp.float32),
            jax.ShapeDtypeStruct((chunks, 1, width), jnp.float32),
        ),
        in_specs=[vmem, vmem, anywhere, anywhere, vmem, vmem],
        out_specs=(vmem, vmem, vmem, vmem),
        scratch_shapes=[
            pltpu.VMEM((units, total_rows, width), jnp.float32),
            unit_buffer,
            unit_buffer,
            pltpu.VMEM((2, total_rows, width), jnp.bfloat16),
            pltpu.VMEM((2, total_rows, width), jnp.bfloat16),
            pltpu.VMEM((slots, model, width), jnp.bfloat16),
            pltpu.VMEM((2, width, model), jnp.bfloat16),
            pltpu.SemaphoreType.DMA((slots,)),
            pltpu.SemaphoreType.DMA((2,)),
            pltpu.SemaphoreType.DMA((2,)),
            unit_sems,
            pltpu.SemaphoreType.DMA((2,)),
            unit_sems,
        ],
        compiler_params=pltpu.CompilerParams(
            collective_id=0, has_side_effects=True, vmem_limit_bytes=63 * 1024 * 1024
        ),
        cost_estimate=pl.CostEstimate(
            flops=6 * total_rows * model * ff_local,
            bytes_accessed=4 * model * ff_local,
            transcendentals=2 * total_rows * ff_local,
        ),
    )(all_tokens, all_grads, w_in, w_out, bias, keep)


def local(tokens, out_grad, w_in, w_out, bias_in, stream_ids, tile_keys):
    col_count = lax.axis_size("col")
    row_index = lax.axis_index("row")
    col_index = lax.axis_index("col")
    ff_local = w_in.shape[1]
    width = 256
    chunks = ff_local // width
    all_tokens, all_grads = (
        lax.all_gather(tokens, "row", axis=0, tiled=True),
        lax.all_gather(out_grad, "row", axis=0, tiled=True),
    )
    tile_count = ff_local // TILE_F
    keep = keep_mask(tile_keys, stream_ids, row_index * tile_count, tile_count, width // TILE_F)
    act, dpre, token_terms, bias_sum = exchange(
        all_tokens, all_grads, w_in, w_out, bias_in.reshape(chunks, 1, width), keep, col_count
    )
    grad_tokens = lax.psum_scatter(
        token_terms, "row", scatter_dimension=0, tiled=True
    ).astype(jnp.bfloat16)
    grad_w_out = lax.dot_general(
        act, all_grads, (((0,), (0,)), ((), ())), preferred_element_type=jnp.float32
    ).astype(jnp.bfloat16)
    grad_w_in = lax.dot_general(
        all_tokens, dpre, (((0,), (0,)), ((), ())), preferred_element_type=jnp.float32
    ).astype(jnp.bfloat16)
    share = ff_local // col_count
    grad_bias_in = lax.all_gather(
        lax.dynamic_slice_in_dim(bias_sum.reshape(ff_local), col_index * share, share, 0),
        "col", axis=0, tiled=True,
    )
    grad_bias_out = jnp.sum(all_grads.astype(jnp.float32), axis=0)
    return (grad_tokens, grad_w_in, grad_w_out, grad_bias_in, grad_bias_out)


def solution(mesh):
    return jax.shard_map(
        local,
        mesh=mesh,
        in_specs=(
            P("row", "col"),
            P("row", "col"),
            P("col", "row"),
            P("row", "col"),
            P("row"),
            P(),
            P(),
        ),
        out_specs=(P("row", "col"), P("col", "row"), P("row", "col"), P("row"), P("col")),
        check_vma=False,
    )
```

time: 514 us -> 345 us (0.67)
  waiting for transfers between devices: 376 us -> 62.8 us
  Pallas kernels: 0 us -> 186 us
  matrix products: 85.6 us -> 30.1 us
  blocking collectives: 0 us -> 13.2 us
    reduce_scatter x3 -> x1, waiting for transfers between devices: 256 us -> 0.01 us  [local(): lax.psum_scatter(token_terms, 'row', scatter_dimension=0, tiled=True)]
    pallas_call x0 -> x1, Pallas kernels: none -> 186 us  [exchange(): pl.pallas_call(functools.partial(exchange_kernel, n, units, slots, 32), o...]
    all_gather x2 -> x0, waiting for transfers between devices: 63.9 us -> none  [the longest x1 63.3 us: local(): lax.all_gather(dpre, 'col', axis=1, tiled=True)]
    dot_general x6 -> x2, matrix products: 85.6 us -> 30.1 us  [the longest x1 15.1 us: local(): lax.dot_general(act, all_grads, (((0,), (0,)), ((), ())), preferred_eleme...]
    all_gather x0 -> x1, blocking collectives: none -> 13.2 us  [local(): lax.all_gather(lax.dynamic_slice_in_dim(bias_sum.reshape(ff_local), col_i...]
    all_gather x1, waiting for transfers between devices: 17.8 us -> 27.2 us  [local(): lax.all_gather(tokens, 'row', axis=0, tiled=True)]
    convert_element_type x1 -> x2, other arithmetic: 1.92 us -> 7.19 us  [the longest x1 5.27 us: keep_mask(): keep.astype(jnp.bfloat16)]
    unnamed x11 -> x12, local copies, waits for them, and re-layouts: 27.7 us -> 25.7 us
  transfers between devices with their start and end apart: 7 -> 3, of which waited for: 7 -> 2; matrix products, arithmetic and copies ran while one was open for 21% -> 18% of each run, Pallas kernels for 0% -> 0%
where the time goes in v1:
time: 345 us; the launch traced here: 344 us
  Pallas kernels  186 us (54%)
  waiting for transfers between devices  62.8 us (18%)
  matrix products  30.1 us (9%)
  local copies, waits for them, and re-layouts  28.2 us (8%)
  between operations  15.8 us (5%)
  blocking collectives  13.2 us (4%)
  other arithmetic  8.44 us (2%)
    pallas_call x1, Pallas kernels, exchange(): pl.pallas_call(functools.partial(exchange_kernel, n, units, slots, 32), o...  186 us
    all_gather x1, waiting for transfers between devices, local(): lax.all_gather(out_grad, 'row', axis=0, tiled=True)  34.2 us
    all_gather x1, waiting for transfers between devices, local(): lax.all_gather(tokens, 'row', axis=0, tiled=True)  27.2 us
    unnamed x12, local copies, waits for them, and re-layouts  25.7 us
    dot_general x1, matrix products, local(): lax.dot_general(act, all_grads, (((0,), (0,)), ((), ())), preferred_eleme...  15.1 us
    dot_general x1, matrix products, local(): lax.dot_general(all_tokens, dpre, (((0,), (0,)), ((), ())), preferred_ele...  15 us
    all_gather x1, blocking collectives, local(): lax.all_gather(lax.dynamic_slice_in_dim(bias_sum.reshape(ff_local), col_i...  13.2 us
  transfers between devices with their start and end apart: 3, of which 2 were waited for; matrix products, arithmetic and copies ran while one was open for 18% of the time, Pallas kernels for 0%

profile of v1, /device:TPU:0, one launch (start us, length us, event | category | flops | bytes accessed | tf_op | source)
XLA Modules:
  0.0 344.3 jit_solution(8916492982173446948)
XLA Ops:
  7.2 0.0 all-gather.4.cloned.1.call-start
  7.2 0.7 all-gather.4.cloned.1.call-update
  7.9 0.0 all-gather.6.cloned.1.call-start
  8.0 0.7 all-gather.6.cloned.1.call-update
  8.7 0.0 reduce-scatter.2.cloned.1.call-start
  8.7 0.1 iota.23
  8.8 0.1 constant_dynamic-slice_fusion
  8.9 0.1 copy.23
  9.0 1.4 fusion.6
  12.3 0.2 copy.21
  12.5 5.3 %fusion.5.keep = bf16[12,512,256]{2,1,0:T(8,128)(2,1)} fusion(s32[256]{0:T(256)S(1)} %iota_bitcast_fusion, s32[512]{0:T(512)S(1)} %iota.23, s32[12,64,2]{2,1,0:T(8,128)S(1)} %copy.21), kind=kLoop, calls=%fused_computation.12 | loop fusion | flops 23592960 | bytes 3154944 | tf_op jit(solution)/shard_map/convert_element_type | solution.py:48
  17.8 27.2 %all-gather.4.cloned.1.call-done.tokens = bf16[512,3072]{1,0:T(8,128)(2,1)} async-done(((bf16[64,3072]{1,0:T(8,128)(2,1)}), bf16[512,3072]{1,0:T(8,128)(2,1)}) %all-gather.4.cloned.1.call-update) | async-done | bytes 3145744 | tf_op jit(solution)/shard_map/all_gather | solution.py:278
  44.9 34.2 %all-gather.6.cloned.1.call-done.grads = bf16[512,3072]{1,0:T(8,128)(2,1)} async-done(((bf16[64,3072]{1,0:T(8,128)(2,1)}), bf16[512,3072]{1,0:T(8,128)(2,1)}) %all-gather.6.cloned.1.call-update) | async-done | bytes 3145744 | tf_op jit(solution)/shard_map/all_gather | solution.py:279
  79.2 185.6 %shard_map.110 = (bf16[512,3072]{1,0:T(8,128)(2,1)}, bf16[512,3072]{1,0:T(8,128)(2,1)}, f32[512,3072]{1,0:T(8,128)}, f32[12,1,256]{2,1,0:T(1,128)}) custom-call(bf16[512,3072]{1,0:T(8,128)(2,1)} %all-gather.4.cloned.1.call-done.tokens, bf16[512,3072]{1,0:T(8,128)(2,1)} %all-gather.6.cloned.1.call-done.grads, bf16[3072,3072]{1,0:T(8,128)(2,1)} %w_in.1, ...), custom_call_target="tpu_custom_call" | custom-call | flops 28991029248 | bytes 37748736 | tf_op jit(solution)/shard_map/pallas_call | solution.py:234
  264.8 0.0 reduce-scatter.2.cloned.1.call-update
  264.8 1.9 copy-done.3
  266.7 15.0 %convert_bitcast_fusion = bf16[3072,3072]{0,1:T(8,128)(2,1)} fusion(bf16[512,3072]{1,0:T(8,128)(2,1)} %get-tuple-element.10, bf16[512,3072]{1,0:T(8,128)(2,1)S(1)} %copy-done.3), kind=kOutput, calls=%fused_computation | convolution fusion | flops 9673113600 | bytes 25165824 | tf_op jit(solution)/shard_map/dot_general | solution.py:292
  281.7 23.2 %copy.22 = bf16[3072,3072]{1,0:T(8,128)(2,1)} copy(bf16[3072,3072]{0,1:T(8,128)(2,1)} %convert_bitcast_fusion) | data formatting | bytes 37748736
  304.9 0.8 dynamic_slice.7
  305.7 13.2 %all-gather = f32[4,1,768]{2,1,0:T(1,128)S(1)} all-gather(f32[1,1,768]{2,1,0:T(1,128)S(1)} %reshape.35), channel_id=1, replica_groups=mesh['row'=8,'col'=4] {'col'}, dimensions={0}, use_global_device_ids=true | all-gather | bytes 15360 | tf_op jit(solution)/shard_map/all_gather | solution.py:296
  318.9 1.2 convert_reduce_fusion
  320.1 15.1 %convolution_convert_fusion = bf16[3072,3072]{1,0:T(8,128)(2,1)} fusion(bf16[512,3072]{1,0:T(8,128)(2,1)} %get-tuple-element.11, bf16[512,3072]{1,0:T(8,128)(2,1)S(1)} %copy-done.2), kind=kOutput, calls=%fused_computation.1 | convolution fusion | flops 9673113600 | bytes 25165824 | tf_op jit(solution)/shard_map/dot_general | solution.py:289
  335.2 1.9 convert_element_type.20
  337.1 0.6 copy.25
  (13 shorter events, 0.0 us)
Async XLA Ops:
  7.2 1.7 copy-start
  7.2 37.8 %all-gather.4.cloned.1.call-start = ((), (), s32[]{:S(2)}) async-start(), calls=%async_computation.1 | async-start | bytes 3538944 | tf_op jit(solution)/shard_map/all_gather | solution.py:278
  7.9 71.3 %all-gather.6.cloned.1.call-start = ((), (), s32[]{:S(2)}) async-start(), calls=%async_computation.2 | async-start | bytes 3538944 | tf_op jit(solution)/shard_map/all_gather | solution.py:279
  8.7 326.6 %reduce-scatter.2.cloned.1.call-start = ((), (), s32[]{:S(2)}) async-start(), calls=%async_computation.3 | async-start | bytes 7077888 | tf_op jit(solution)/shard_map/reduce_scatter | solution.py:286
  264.8 1.9 copy-start.3
  281.7 37.2 %copy-start.2 = (bf16[512,3072]{1,0:T(8,128)(2,1)S(1)}, bf16[512,3072]{1,0:T(8,128)(2,1)}, u32[]{:S(2)}) copy-start(bf16[512,3072]{1,0:T(8,128)(2,1)} %all-gather.6.cloned.1.call-done.grads) | copy-start | bytes 9437188
  320.1 17.6 %copy-start.1 = (s32[64,192]{1,0:T(8,128)S(1)}, s32[64,192]{1,0:T(8,128)}, u32[]{:S(2)}) copy-start(s32[64,192]{1,0:T(8,128)} %param.13) | copy-start | bytes 147460
Sparse Core Ops, SparseCore 0:
  9.9 35.0 all-gather.3
  46.8 32.3 all-gather.5
  264.9 61.5 reduce-scatter.1

commit v2 on v1

--- a/solution.py
+++ b/solution.py
@@ -49,18 +49,19 @@
 
 
 def exchange_kernel(
-    n, units, slots, rows,
+    n, lag, units, slots, rows,
     tokens, grads, w_in, w_out, bias, keep,
-    act, dpre, acc, bias_sum,
+    act, dpre, acc, bias_out,
     own, from_left, from_right, to_right, to_left, in_ring, out_ring,
     in_sem, out_sem, right_send, right_recv, left_send, left_recv,
+    bias_sum, bias_landed, bias_send, bias_recv,
 ):
     me = lax.axis_index("col")
     right, left = lax.rem(me + 1, n), lax.rem(me + n - 1, n)
     total_rows, width = own.shape[1], own.shape[2]
     model = in_ring.shape[1]
     chunks = units // 2
-    far = jnp.maximum(me, n - 1 - me)
+    far = jnp.maximum(me, n - 1 - me) * lag
 
     def fetch_in(c):
         slot = lax.rem(c, slots)
@@ -137,26 +138,21 @@
         cols = pl.ds(pl.multiple_of(c * width, width), width)
         shift = bias[c]
 
-        def add_arrived(q):
-            @pl.when(me > 0)
-            def _():
-                own[q] += from_left[q].astype(jnp.float32)
-
-            @pl.when(me < n - 1)
-            def _():
-                own[q] += from_right[q].astype(jnp.float32)
-
-        add_arrived(2 * c)
-        add_arrived(2 * c + 1)
+        def whole(q, at):
+            return (
+                own[q, at, :]
+                + from_left[q, at, :].astype(jnp.float32)
+                + from_right[q, at, :].astype(jnp.float32)
+            )
 
         def block(k, total):
             at = pl.ds(pl.multiple_of(k * rows, rows), rows)
-            pre = own[2 * c, at, :] + shift
+            pre = whole(2 * c, at) + shift
             scaled = keep[c, at, :].astype(jnp.float32) * (1.0 / 0.9)
             cdf = 0.5 * (1.0 + lax.erf(pre * 0.7071067811865476))
             act[at, cols] = (pre * cdf * scaled).astype(act.dtype)
             slope = cdf + pre * jnp.exp(-0.5 * pre * pre) * 0.3989422804014327
-            part = (own[2 * c + 1, at, :] * scaled * slope).astype(dpre.dtype)
+            part = (whole(2 * c + 1, at) * scaled * slope).astype(dpre.dtype)
             dpre[at, cols] = part
             return total + jnp.sum(part.astype(jnp.float32), axis=0, keepdims=True)
 
@@ -179,16 +175,34 @@
     fetch_out(0).start()
     barrier = pltpu.get_barrier_semaphore()
 
-    for peer in (left, right):
-        pl.semaphore_signal(barrier, inc=1, device_id={"col": peer}, device_id_type=MESH)
+    for k in range(1, n):
+        pl.semaphore_signal(
+            barrier, inc=1, device_id={"col": lax.rem(me + k, n)}, device_id_type=MESH
+        )
+
+    def clear(buffer):
+        def one(q, carry):
+            buffer[q] = jnp.zeros(buffer.shape[1:], buffer.dtype)
+            return carry
+
+        lax.fori_loop(0, units, one, 0)
+
+    @pl.when(me == 0)
+    def _():
+        clear(from_left)
+
+    @pl.when(me == n - 1)
+    def _():
+        clear(from_right)
+
     acc[...] = jnp.zeros_like(acc)
     own_unit(0)
 
-    pl.semaphore_wait(barrier, 2)
+    pl.semaphore_wait(barrier, n - 1)
 
     def step(s, carry):
-        right_unit = s - me
-        left_unit = s - (n - 1 - me)
+        right_unit = s - me * lag
+        left_unit = s - (n - 1 - me) * lag
         done = s - far
 
         @pl.when((right_unit >= 0) & (right_unit < units))
@@ -203,13 +217,13 @@
         def _():
             own_unit(s + 1)
 
-        @pl.when((done >= 0) & (done < units) & (lax.rem(done + 2 * n, 2) == 1))
+        @pl.when((done >= 0) & (done < units) & (lax.rem(done + 2 * n * lag, 2) == 1))
         def _():
             finish(done // 2)
 
         return carry
 
-    lax.fori_loop(0, units + n - 1, step, 0)
+    lax.fori_loop(0, units + (n - 1) * lag, step, 0)
 
     for q in (units - 2, units - 1):
         @pl.when(me < n - 1)
@@ -219,6 +233,26 @@
         @pl.when(me > 0)
         def _():
             send_left(q).wait_send()
+
+    def share_bias(k):
+        return pltpu.make_async_remote_copy(
+            src_ref=bias_sum, dst_ref=bias_landed,
+            send_sem=bias_send.at[k], recv_sem=bias_recv,
+            device_id={"col": lax.rem(me + k, n)}, device_id_type=MESH,
+        )
+
+    @pl.when(me == 0)
+    def _():
+        for k in range(1, n):
+            share_bias(k).start()
+        bias_out[...] = bias_sum[...]
+        for k in range(1, n):
+            share_bias(k).wait_send()
+
+    @pl.when(me > 0)
+    def _():
+        share_bias(1).wait_recv()
+        bias_out[...] = bias_landed[...]
 
 
 def exchange(all_tokens, all_grads, w_in, w_out, bias, keep, n):
@@ -226,13 +260,14 @@
     ff_local = w_in.shape[1]
     chunks, _, width = keep.shape
     units = 2 * chunks
-    slots = n // 2 + 3
+    lag = 2
+    slots = (n - 1) * lag // 2 + 3
     vmem = pl.BlockSpec(memory_space=pltpu.VMEM)
     anywhere = pl.BlockSpec(memory_space=pl.ANY)
     unit_buffer = pltpu.VMEM((units, total_rows, width), jnp.bfloat16)
     unit_sems = pltpu.SemaphoreType.DMA((units,))
     return pl.pallas_call(
-        functools.partial(exchange_kernel, n, units, slots, 32),
+        functools.partial(exchange_kernel, n, lag, units, slots, 32),
         out_shape=(
             jax.ShapeDtypeStruct((total_rows, ff_local), jnp.bfloat16),
             jax.ShapeDtypeStruct((total_rows, ff_local), jnp.bfloat16),
@@ -255,6 +290,10 @@
             unit_sems,
             pltpu.SemaphoreType.DMA((2,)),
             unit_sems,
+            pltpu.VMEM((chunks, 1, width), jnp.float32),
+            pltpu.VMEM((chunks, 1, width), jnp.float32),
+            pltpu.SemaphoreType.DMA((n,)),
+            pltpu.SemaphoreType.DMA,
         ],
         compiler_params=pltpu.CompilerParams(
             collective_id=0, has_side_effects=True, vmem_limit_bytes=63 * 1024 * 1024
@@ -267,36 +306,143 @@
     )(all_tokens, all_grads, w_in, w_out, bias, keep)
 
 
+def gather_kernel(count, tokens, grads, all_tokens, all_grads,
+                  here, far_send, far_recv, mate_send, mate_recv):
+    me = lax.axis_index("row")
+    mate = me + 1 - 2 * lax.rem(me, 2)
+    half = count // 2
+    pairs = ((tokens, all_tokens), (grads, all_grads))
+    barrier = pltpu.get_barrier_semaphore()
+    for k in range(1, half):
+        pl.semaphore_signal(
+            barrier, inc=1, device_id={"row": lax.rem(me + 2 * k, count)}, device_id_type=MESH
+        )
+    pl.semaphore_signal(barrier, inc=1, device_id={"row": mate}, device_id_type=MESH)
+    keeps = [
+        pltpu.make_async_copy(src, dst.at[me], here.at[a]) for a, (src, dst) in enumerate(pairs)
+    ]
+    for copy in keeps:
+        copy.start()
+    pl.semaphore_wait(barrier, half)
+
+    def to_far(a, k):
+        src, dst = pairs[a]
+        return pltpu.make_async_remote_copy(
+            src_ref=src, dst_ref=dst.at[me],
+            send_sem=far_send.at[a, k], recv_sem=far_recv.at[a, k],
+            device_id={"row": lax.rem(me + 2 * k, count)}, device_id_type=MESH,
+        )
+
+    def to_mate(a, k):
+        src, dst = pairs[a]
+        origin = lax.rem(me + count - 2 * k, count)
+        return pltpu.make_async_remote_copy(
+            src_ref=src if k == 0 else dst.at[origin], dst_ref=dst.at[origin],
+            send_sem=mate_send.at[a, k], recv_sem=mate_recv.at[a, k],
+            device_id={"row": mate}, device_id_type=MESH,
+        )
+
+    for a in range(2):
+        for k in range(1, half):
+            to_far(a, k).start()
+    for a in range(2):
+        to_mate(a, 0).start()
+    for a in range(2):
+        for k in range(1, half):
+            to_far(a, k).wait_recv()
+            to_mate(a, k).start()
+    for a in range(2):
+        for k in range(1, half):
+            to_far(a, k).wait_send()
+        for k in range(half):
+            to_mate(a, k).wait()
+        keeps[a].wait()
+
+
+def gather_rows(tokens, grads):
+    count = lax.axis_size("row")
+    rows, model = tokens.shape
+    anywhere = pl.BlockSpec(memory_space=pl.ANY)
+    shape = jax.ShapeDtypeStruct((count, rows, model), tokens.dtype)
+    sems = pltpu.SemaphoreType.DMA((2, count // 2))
+    all_tokens, all_grads = pl.pallas_call(
+        functools.partial(gather_kernel, count),
+        out_shape=(shape, shape),
+        in_specs=[anywhere, anywhere],
+        out_specs=(anywhere, anywhere),
+        scratch_shapes=[pltpu.SemaphoreType.DMA((2,)), sems, sems, sems, sems],
+        compiler_params=pltpu.CompilerParams(collective_id=1, has_side_effects=True),
+    )(tokens, grads)
+    return (all_tokens.reshape(count * rows, model), all_grads.reshape(count * rows, model))
+
+
+def weight_grad_kernel(left, right, out):
+    columns = out.shape[1]
+    step = 512 if columns % 512 == 0 else columns
+    for start in range(0, columns, step):
+        out[:, start:start + step] = lax.dot_general(
+            left[...], right[:, start:start + step], (((0,), (0,)), ((), ())),
+            preferred_element_type=jnp.float32,
+        ).astype(out.dtype)
+
+
+def weight_grad(left, right):
+    tokens, rows = left.shape
+    columns = right.shape[1]
+    tile = 256
+    return pl.pallas_call(
+        weight_grad_kernel,
+        out_shape=jax.ShapeDtypeStruct((rows, columns), jnp.bfloat16),
+        grid=(rows // tile,),
+        in_specs=[
+            pl.BlockSpec((tokens, tile), lambda i: (0, i)),
+            pl.BlockSpec((tokens, columns), lambda i: (0, 0)),
+        ],
+        out_specs=pl.BlockSpec((tile, columns), lambda i: (i, 0)),
+        compiler_params=pltpu.CompilerParams(vmem_limit_bytes=32 * 1024 * 1024),
+        cost_estimate=pl.CostEstimate(
+            flops=2 * tokens * rows * columns,
+            bytes_accessed=2 * (rows * columns + tokens * (rows + columns)),
+            transcendentals=0,
+        ),
+    )(left, right)
+
+
+def scatter_rows(terms):
+    count = lax.axis_size("row")
+    me = lax.axis_index("row")
+    half = count // 2
+    group, side = me // 2, lax.rem(me, 2)
+    terms = terms.reshape(half, 2, terms.shape[0] // count, terms.shape[1])
+    other = lax.dynamic_index_in_dim(terms, 1 - side, 1, keepdims=False).astype(jnp.bfloat16)
+    other = lax.ppermute(other, "row", [(r, r + 1 - 2 * (r % 2)) for r in range(count)])
+    mine = lax.dynamic_index_in_dim(terms, side, 1, keepdims=False) + other.astype(jnp.float32)
+    total = lax.dynamic_index_in_dim(mine, group, 0, keepdims=False)
+    for k in range(1, half):
+        block = lax.dynamic_index_in_dim(mine, lax.rem(group + k, half), 0, keepdims=False)
+        block = lax.ppermute(
+            block.astype(jnp.bfloat16), "row", [(r, (r + 2 * k) % count) for r in range(count)]
+        )
+        total = total + block.astype(jnp.float32)
+    return total.astype(jnp.bfloat16)
+
+
 def local(tokens, out_grad, w_in, w_out, bias_in, stream_ids, tile_keys):
     col_count = lax.axis_size("col")
     row_index = lax.axis_index("row")
-    col_index = lax.axis_index("col")
     ff_local = w_in.shape[1]
     width = 256
     chunks = ff_local // width
-    all_tokens, all_grads = (
-        lax.all_gather(tokens, "row", axis=0, tiled=True),
-        lax.all_gather(out_grad, "row", axis=0, tiled=True),
-    )
+    all_tokens, all_grads = gather_rows(tokens, out_grad)
     tile_count = ff_local // TILE_F
     keep = keep_mask(tile_keys, stream_ids, row_index * tile_count, tile_count, width // TILE_F)
     act, dpre, token_terms, bias_sum = exchange(
         all_tokens, all_grads, w_in, w_out, bias_in.reshape(chunks, 1, width), keep, col_count
     )
-    grad_tokens = lax.psum_scatter(
-        token_terms, "row", scatter_dimension=0, tiled=True
-    ).astype(jnp.bfloat16)
-    grad_w_out = lax.dot_general(
-        act, all_grads, (((0,), (0,)), ((), ())), preferred_element_type=jnp.float32
-    ).astype(jnp.bfloat16)
-    grad_w_in = lax.dot_general(
-        all_tokens, dpre, (((0,), (0,)), ((), ())), preferred_element_type=jnp.float32
-    ).astype(jnp.bfloat16)
-    share = ff_local // col_count
-    grad_bias_in = lax.all_gather(
-        lax.dynamic_slice_in_dim(bias_sum.reshape(ff_local), col_index * share, share, 0),
-        "col", axis=0, tiled=True,
-    )
+    grad_tokens = scatter_rows(token_terms)
+    grad_w_out = weight_grad(act, all_grads)
+    grad_w_in = weight_grad(all_tokens, dpre)
+    grad_bias_in = bias_sum.reshape(ff_local)
     grad_bias_out = jnp.sum(all_grads.astype(jnp.float32), axis=0)
     return (grad_tokens, grad_w_in, grad_w_out, grad_bias_in, grad_bias_out)
 

time: 345 us -> 276 us (0.80)
  waiting for transfers between devices: 62.8 us -> 2.79 us
  Pallas kernels: 186 us -> 243 us
  matrix products: 30.1 us -> 0 us
  local copies, waits for them, and re-layouts: 28.2 us -> 12.8 us
  blocking collectives: 13.2 us -> 0 us
  between operations: 15.8 us -> 2.69 us
    all_gather x2 -> x0, waiting for transfers between devices: 61.4 us -> none  [the longest x1 34.2 us: local(): lax.all_gather(out_grad, 'row', axis=0, tiled=True)]
    pallas_call x1 -> x4, Pallas kernels: 186 us -> 243 us  [the longest x1 173 us: exchange(): pl.pallas_call(functools.partial(exchange_kernel, n, lag, units, slots, 3...]
    dot_general x2 -> x0, matrix products: 30.1 us -> none  [the longest x1 15.1 us: local(): lax.dot_general(act, all_grads, (((0,), (0,)), ((), ())), preferred_eleme...]
    unnamed x12 -> x20, local copies, waits for them, and re-layouts: 25.7 us -> 6.8 us
    all_gather x1 -> x0, blocking collectives: 13.2 us -> none  [local(): lax.all_gather(lax.dynamic_slice_in_dim(bias_sum.reshape(ff_local), col_i...]
    convert_element_type x0 -> x2, local copies, waits for them, and re-layouts: none -> 4.31 us  [the longest x1 3.26 us: scatter_rows(): lax.dynamic_index_in_dim(terms, 1 - side, 1, keepdims=False)]
  transfers between devices with their start and end apart: 3 -> 4, of which waited for: 2 -> 1; matrix products, arithmetic and copies ran while one was open for 18% -> 0% of each run, Pallas kernels for 0% -> 10%
where the time goes in v2:
time: 276 us
  Pallas kernels  243 us (88%)
  local copies, waits for them, and re-layouts  12.8 us (5%)
  other arithmetic  11 us (4%)
  starting transfers between devices  3.44 us (1%)
  waiting for transfers between devices  2.79 us (1%)
    pallas_call x1, Pallas kernels, exchange(): pl.pallas_call(functools.partial(exchange_kernel, n, lag, units, slots, 3...  173 us
    pallas_call x1, Pallas kernels, gather_rows(): pl.pallas_call(functools.partial(gather_kernel, count), out_shape=(shape,...  41.5 us
    pallas_call x2, Pallas kernels, weight_grad(): pl.pallas_call(weight_grad_kernel, out_shape=jax.ShapeDtypeStruct((rows,...  28.6 us
    unnamed x20, local copies, waits for them, and re-layouts  6.8 us
  transfers between devices with their start and end apart: 4, of which 1 were waited for; matrix products, arithmetic and copies ran while one was open for 0% of the time, Pallas kernels for 10%

profile of v2, /device:TPU:0, one launch (start us, length us, event | category | flops | bytes accessed | tf_op | source)
XLA Modules:
  0.0 276.1 jit_solution(4346263647347117203)
XLA Ops:
  0.7 0.1 iota.23
  0.8 0.7 copy-done
  1.5 0.1 constant_dynamic-slice_fusion
  1.6 0.1 copy.20
  1.6 1.4 fusion.13
  4.9 0.2 copy.18
  5.2 41.5 %shard_map.110 = (bf16[8,64,3072]{2,1,0:T(8,128)(2,1)}, bf16[8,64,3072]{2,1,0:T(8,128)(2,1)}) custom-call(bf16[64,3072]{1,0:T(8,128)(2,1)} %tokens.1, bf16[64,3072]{1,0:T(8,128)(2,1)} %grads.1), custom_call_target="tpu_custom_call" | custom-call | tf_op jit(solution)/shard_map/pallas_call | solution.py:368
  46.7 5.3 %fusion.5.keep = bf16[12,512,256]{2,1,0:T(8,128)(2,1)} fusion(s32[256]{0:T(256)S(1)} %iota_bitcast_fusion, s32[512]{0:T(512)S(1)} %iota.23, s32[12,64,2]{2,1,0:T(8,128)S(1)} %copy.18), kind=kLoop, calls=%fused_computation.10 | loop fusion | flops 23592960 | bytes 3154944 | tf_op jit(solution)/shard_map/convert_element_type | solution.py:48
  52.0 173.3 %shard_map.111 = (bf16[512,3072]{1,0:T(8,128)(2,1)}, bf16[512,3072]{1,0:T(8,128)(2,1)}, f32[512,3072]{1,0:T(8,128)}, f32[12,1,256]{2,1,0:T(1,128)}) custom-call(bf16[512,3072]{1,0:T(8,128)(2,1)} %bitcast.41, bf16[512,3072]{1,0:T(8,128)(2,1)} %bitcast.39, bf16[3072,3072]{1,0:T(8,128)(2,1)} %w_in.1, bf16[3072,3072]{1,0:T(8,128)(2,1)} %w_out.1, ...), custom_call_target="tpu_custom_call" | custom-call | flops 28991029248 | bytes 37748736 | tf_op jit(solution)/shard_map/pallas_call | solution.py:269
  225.3 3.3 %fusion.6 = bf16[4,64,3072]{2,1,0:T(8,128)(2,1)} fusion(f32[4,2,64,3072]{3,2,1,0:T(8,128)} %bitcast.43, s32[]{:T(128)S(6)} %select_n.30), kind=kLoop, calls=%fused_computation.13 | loop fusion | bytes 3145732 | tf_op jit(solution)/shard_map/convert_element_type | solution.py:417
  228.5 1.9 copy-done.3
  230.4 1.9 copy-done.5
  232.3 14.3 %shard_map.112 = bf16[3072,3072]{1,0:T(8,128)(2,1)} custom-call(bf16[512,3072]{1,0:T(8,128)(2,1)S(1)} %bitcast.42, bf16[512,3072]{1,0:T(8,128)(2,1)S(1)} %copy-done.5), custom_call_target="tpu_custom_call" | custom-call | flops 9663676416 | bytes 25165824 | tf_op jit(solution)/shard_map/pallas_call | solution.py:393
  246.6 2.0 bitcast_add_fusion.1
  248.7 1.6 copy-done.6
  250.3 1.1 fusion.10
  251.3 1.8 collective-permute-start.3
  253.1 0.6 collective-permute-start.2
  253.7 1.1 collective-permute-start.1
  254.8 14.3 %shard_map.113 = bf16[3072,3072]{1,0:T(8,128)(2,1)} custom-call(bf16[512,3072]{1,0:T(8,128)(2,1)S(1)} %copy-done.4, bf16[512,3072]{1,0:T(8,128)(2,1)S(1)} %bitcast.40), custom_call_target="tpu_custom_call" | custom-call | flops 9663676416 | bytes 25165824 | tf_op jit(solution)/shard_map/pallas_call | solution.py:393
  269.1 1.2 convert_reduce_fusion
  270.3 2.8 %collective-permute-done.2 = bf16[64,3072]{1,0:T(8,128)(2,1)} collective-permute-done((bf16[64,3072]{1,0:T(8,128)(2,1)}, bf16[64,3072]{1,0:T(8,128)(2,1)}, u32[]{:S(2)}, u32[]{:S(2)}) %collective-permute-start.2) | collective-permute-done | bytes 393248 | tf_op jit(solution)/shard_map/ppermute | solution.py:423
  273.1 2.4 fusion.9
  275.5 0.6 copy.23
  (22 shorter events, 0.1 us)
Async XLA Ops:
  0.6 0.8 copy-start
  228.5 18.1 %collective-permute-start = (bf16[4,64,3072]{2,1,0:T(8,128)(2,1)}, bf16[4,64,3072]{2,1,0:T(8,128)(2,1)}, u32[]{:S(2)}, u32[]{:S(2)}) collective-permute-start(bf16[4,64,3072]{2,1,0:T(8,128)(2,1)} %fusion.6), channel_id=1, source_target_pairs={{0,4},{4,0},{8,12},{12,8},{16,20},{20,16},{24,28},{28,24},{1,5},{5... | collective-permute-start | bytes 4718600 | tf_op jit(solution)/shard_map/ppermute | solution.py:418
  228.5 1.9 copy-start.3
  230.4 1.9 copy-start.5
  232.3 14.3 %copy-start.7 = (f32[512,3072]{1,0:T(8,128)S(1)}, f32[512,3072]{1,0:T(8,128)}, u32[]{:S(2)}) copy-start(f32[512,3072]{1,0:T(8,128)} %get-tuple-element.13) | copy-start | bytes 18874372
  246.6 8.2 %copy-start.2 = (bf16[8,64,3072]{2,1,0:T(8,128)(2,1)S(1)}, bf16[8,64,3072]{2,1,0:T(8,128)(2,1)}, u32[]{:S(2)}) copy-start(bf16[8,64,3072]{2,1,0:T(8,128)(2,1)} %get-tuple-element.12) | copy-start | bytes 9437188
  246.6 8.2 %copy-start.4 = (bf16[512,3072]{1,0:T(8,128)(2,1)S(1)}, bf16[512,3072]{1,0:T(8,128)(2,1)}, u32[]{:S(2)}) copy-start(bf16[512,3072]{1,0:T(8,128)(2,1)} %get-tuple-element.15.left) | copy-start | bytes 9437188
  248.7 1.6 copy-start.6
  251.3 19.0 %collective-permute-start.3 = (bf16[64,3072]{1,0:T(8,128)(2,1)}, bf16[64,3072]{1,0:T(8,128)(2,1)}, u32[]{:S(2)}, u32[]{:S(2)}) collective-permute-start(bf16[64,3072]{1,0:T(8,128)(2,1)} %get-tuple-element.18), channel_id=1, source_target_pairs={{0,24},{4,28},{8,0},{12,4},{16,8},{20,12},{24,16},{28,20},{1,25},{... | collective-permute-start | bytes 1179656 | tf_op jit(solution)/shard_map/ppermute | solution.py:423
  253.1 20.0 %collective-permute-start.2 = (bf16[64,3072]{1,0:T(8,128)(2,1)}, bf16[64,3072]{1,0:T(8,128)(2,1)}, u32[]{:S(2)}, u32[]{:S(2)}) collective-permute-start(bf16[64,3072]{1,0:T(8,128)(2,1)} %get-tuple-element.19), channel_id=1, source_target_pairs={{0,16},{4,20},{8,24},{12,28},{16,0},{20,4},{24,8},{28,12},{1,17},{... | collective-permute-start | bytes 1179656 | tf_op jit(solution)/shard_map/ppermute | solution.py:423
  253.7 19.4 %collective-permute-start.1 = (bf16[64,3072]{1,0:T(8,128)(2,1)}, bf16[64,3072]{1,0:T(8,128)(2,1)}, u32[]{:S(2)}, u32[]{:S(2)}) collective-permute-start(bf16[64,3072]{1,0:T(8,128)(2,1)} %get-tuple-element.17), channel_id=1, source_target_pairs={{0,8},{4,12},{8,16},{12,20},{16,24},{20,28},{24,0},{28,4},{1,9},{5... | collective-permute-start | bytes 1179656 | tf_op jit(solution)/shard_map/ppermute | solution.py:423
  254.8 20.7 %copy-start.8 = (f32[12,1,256]{2,1,0:T(1,128)S(1)}, f32[12,1,256]{2,1,0:T(1,128)}, u32[]{:S(2)}) copy-start(f32[12,1,256]{2,1,0:T(1,128)} %get-tuple-element.16) | copy-start | bytes 36868
  254.8 21.3 %copy-start.1 = (s32[64,192]{1,0:T(8,128)S(1)}, s32[64,192]{1,0:T(8,128)}, u32[]{:S(2)}) copy-start(s32[64,192]{1,0:T(8,128)} %param.13) | copy-start | bytes 147460

commit v3 on v2

--- a/solution.py
+++ b/solution.py
@@ -24,28 +24,45 @@
     return lax.shift_right_logical(value, jnp.full(value.shape, count, jnp.int32))
 
 
-def keep_mask(tile_keys, stream_ids, first_tile, tile_count, per_chunk):
+def salted_keys(tile_keys, stream_ids, first_tile, tile_count):
     salt = (
         stream_ids[0] * jnp.int32(mix_one)
         ^ stream_ids[1] * jnp.int32(mix_two)
         ^ stream_ids[2] * jnp.int32(mix_three)
     )
-    token_tiles = tile_keys.shape[0]
-    chunks = tile_count // per_chunk
-    keys = lax.dynamic_slice_in_dim(tile_keys, first_tile, tile_count, 1) ^ salt
-    keys = keys.reshape(token_tiles, chunks, per_chunk).transpose(1, 0, 2)
-    shape = (chunks, token_tiles, TILE_T, per_chunk, TILE_F)
-    offset = lax.broadcasted_iota(jnp.int32, shape, 2) * TILE_F + lax.broadcasted_iota(
-        jnp.int32, shape, 4
-    )
-    value = keys[:, :, None, :, None] + offset * jnp.int32(golden)
+    return lax.dynamic_slice_in_dim(tile_keys, first_tile, tile_count, 1) ^ salt
+
+
+def keep_tile(key, offset):
+    value = key + offset
     value = value ^ shift_down(value, 16)
     value = value * jnp.int32(mult_one)
     value = value ^ shift_down(value, 15)
     value = value * jnp.int32(mult_two)
     value = value ^ shift_down(value, 16)
-    keep = (shift_down(value, 8) & jnp.int32(1023)) < jnp.int32(922)
-    return keep.astype(jnp.bfloat16).reshape(chunks, token_tiles * TILE_T, per_chunk * TILE_F)
+    kept = (shift_down(value, 8) & jnp.int32(1023)) < jnp.int32(922)
+    return jnp.where(kept, 1.0, 0.0)
+
+
+def write_keep(keys, keep):
+    token_tiles, tile_count = keys.shape
+    per_chunk = keep.shape[2] // TILE_F
+    tile = (TILE_T, TILE_F)
+    offset = (
+        lax.broadcasted_iota(jnp.int32, tile, 0) * TILE_F + lax.broadcasted_iota(jnp.int32, tile, 1)
+    ) * jnp.int32(golden)
+
+    def pair(t, carry):
+        at = pl.ds(pl.multiple_of(t * 2 * TILE_T, 2 * TILE_T), 2 * TILE_T)
+        for j in range(tile_count):
+            start = j % per_chunk * TILE_F
+            both = [keep_tile(keys[2 * t + half, j], offset) for half in range(2)]
+            keep[j // per_chunk, at, start:start + TILE_F] = jnp.concatenate(both, 0).astype(
+                keep.dtype
+            )
+        return carry
+
+    lax.fori_loop(0, token_tiles // 2, pair, 0)
 
 
 def exchange_kernel(
@@ -306,7 +323,7 @@
     )(all_tokens, all_grads, w_in, w_out, bias, keep)
 
 
-def gather_kernel(count, tokens, grads, all_tokens, all_grads,
+def gather_kernel(count, tokens, grads, keys, all_tokens, all_grads, keep,
                   here, far_send, far_recv, mate_send, mate_recv):
     me = lax.axis_index("row")
     mate = me + 1 - 2 * lax.rem(me, 2)
@@ -347,6 +364,7 @@
             to_far(a, k).start()
     for a in range(2):
         to_mate(a, 0).start()
+    write_keep(keys, keep)
     for a in range(2):
         for k in range(1, half):
             to_far(a, k).wait_recv()
@@ -359,21 +377,25 @@
         keeps[a].wait()
 
 
-def gather_rows(tokens, grads):
+def gather_rows(tokens, grads, keys, width):
     count = lax.axis_size("row")
     rows, model = tokens.shape
     anywhere = pl.BlockSpec(memory_space=pl.ANY)
     shape = jax.ShapeDtypeStruct((count, rows, model), tokens.dtype)
     sems = pltpu.SemaphoreType.DMA((2, count // 2))
-    all_tokens, all_grads = pl.pallas_call(
+    kept = (keys.shape[1] * TILE_F // width, count * rows, width)
+    all_tokens, all_grads, keep = pl.pallas_call(
         functools.partial(gather_kernel, count),
-        out_shape=(shape, shape),
-        in_specs=[anywhere, anywhere],
-        out_specs=(anywhere, anywhere),
+        out_shape=(shape, shape, jax.ShapeDtypeStruct(kept, jnp.bfloat16)),
+        in_specs=[anywhere, anywhere, pl.BlockSpec(memory_space=pltpu.SMEM)],
+        out_specs=(anywhere, anywhere, pl.BlockSpec(memory_space=pltpu.VMEM)),
         scratch_shapes=[pltpu.SemaphoreType.DMA((2,)), sems, sems, sems, sems],
-        compiler_params=pltpu.CompilerParams(collective_id=1, has_side_effects=True),
-    )(tokens, grads)
-    return (all_tokens.reshape(count * rows, model), all_grads.reshape(count * rows, model))
+        compiler_params=pltpu.CompilerParams(
+            collective_id=1, has_side_effects=True, vmem_limit_bytes=32 * 1024 * 1024
+        ),
+    )(tokens, grads, keys)
+    whole = (count * rows, model)
+    return (all_tokens.reshape(whole), all_grads.reshape(whole), keep)
 
 
 def weight_grad_kernel(left, right, out):
@@ -433,9 +455,9 @@
     ff_local = w_in.shape[1]
     width = 256
     chunks = ff_local // width
-    all_tokens, all_grads = gather_rows(tokens, out_grad)
     tile_count = ff_local // TILE_F
-    keep = keep_mask(tile_keys, stream_ids, row_index * tile_count, tile_count, width // TILE_F)
+    keys = salted_keys(tile_keys, stream_ids, row_index * tile_count, tile_count)
+    all_tokens, all_grads, keep = gather_rows(tokens, out_grad, keys, width)
     act, dpre, token_terms, bias_sum = exchange(
         all_tokens, all_grads, w_in, w_out, bias_in.reshape(chunks, 1, width), keep, col_count
     )

time: 276 us -> 277 us (level)
  other arithmetic: 11 us -> 6.61 us
  local copies, waits for them, and re-layouts: 12.8 us -> 17 us
    convert_element_type x1 -> x0, other arithmetic: 5.27 us -> none  [keep_mask(): keep.astype(jnp.bfloat16)]
    unnamed x20 -> x25, local copies, waits for them, and re-layouts: 6.8 us -> 11.2 us
where the time goes in v3:
time: 277 us; the launch traced here: 276 us
  Pallas kernels  244 us (88%)
  local copies, waits for them, and re-layouts  17 us (6%)
  other arithmetic  6.61 us (2%)
  starting transfers between devices  3.46 us (1%)
  waiting for transfers between devices  2.87 us (1%)
    pallas_call x1, Pallas kernels, exchange(): pl.pallas_call(functools.partial(exchange_kernel, n, lag, units, slots, 3...  173 us
    pallas_call x1, Pallas kernels, gather_rows(): pl.pallas_call(functools.partial(gather_kernel, count), out_shape=(shape,...  41.8 us
    pallas_call x2, Pallas kernels, weight_grad(): pl.pallas_call(weight_grad_kernel, out_shape=jax.ShapeDtypeStruct((rows,...  28.5 us
    unnamed x25, local copies, waits for them, and re-layouts  11.2 us
  transfers between devices with their start and end apart: 4, of which 1 were waited for; matrix products, arithmetic and copies ran while one was open for 0% of the time, Pallas kernels for 10%

profile of v3, /device:TPU:0, one launch (start us, length us, event | category | flops | bytes accessed | tf_op | source)
XLA Modules:
  0.0 276.2 jit_solution(12478674128275466294)
XLA Ops:
  0.6 1.4 fusion.7
  3.9 0.9 dynamic-slice_xor_fusion.keys
  4.9 1.0 copy-done.2
  5.9 1.0 copy-done.3
  6.9 41.8 %shard_map.110 = (bf16[8,64,3072]{2,1,0:T(8,128)(2,1)S(1)}, bf16[8,64,3072]{2,1,0:T(8,128)(2,1)S(1)}, bf16[12,512,256]{2,1,0:T(8,128)(2,1)S(1)}) custom-call(bf16[64,3072]{1,0:T(8,128)(2,1)S(1)} %copy-done.2, bf16[64,3072]{1,0:T(8,128)(2,1)S(1)} %copy-done.3, s32[64,24]{1,0:T(8,128)S(1)} %dynamic-slice_xor_fusion.keys), custom_call_target="tpu_custom_call" | custom-call | tf_op jit(solution)/shard_map/pallas_call | solution.py:387
  48.7 1.7 copy-done
  50.4 1.7 copy-done.4
  52.1 1.7 copy-done.6
  53.7 173.3 %shard_map.111 = (bf16[512,3072]{1,0:T(8,128)(2,1)}, bf16[512,3072]{1,0:T(8,128)(2,1)}, f32[512,3072]{1,0:T(8,128)}, f32[12,1,256]{2,1,0:T(1,128)}) custom-call(bf16[512,3072]{1,0:T(8,128)(2,1)} %bitcast.30, bf16[512,3072]{1,0:T(8,128)(2,1)} %bitcast.28, bf16[3072,3072]{1,0:T(8,128)(2,1)} %w_in.1, bf16[3072,3072]{1,0:T(8,128)(2,1)} %w_out.1, ...), custom_call_target="tpu_custom_call" | custom-call | flops 28991029248 | bytes 37748736 | tf_op jit(solution)/shard_map/pallas_call | solution.py:286
  227.0 0.0 copy-start.5
  227.0 3.4 %fusion = bf16[4,64,3072]{2,1,0:T(8,128)(2,1)} fusion(f32[4,2,64,3072]{3,2,1,0:T(8,128)} %bitcast.32, s32[]{:T(128)S(6)} %select_n.30), kind=kLoop, calls=%fused_computation.3 | loop fusion | bytes 3145732 | tf_op jit(solution)/shard_map/convert_element_type | solution.py:439
  230.5 1.9 copy-done.8
  232.4 14.3 %shard_map.112 = bf16[3072,3072]{1,0:T(8,128)(2,1)} custom-call(bf16[512,3072]{1,0:T(8,128)(2,1)S(1)} %bitcast.31, bf16[512,3072]{1,0:T(8,128)(2,1)S(1)} %copy-done.8), custom_call_target="tpu_custom_call" | custom-call | flops 9663676416 | bytes 25165824 | tf_op jit(solution)/shard_map/pallas_call | solution.py:415
  246.7 2.0 bitcast_add_fusion
  248.7 1.6 copy-done.9
  250.4 1.0 fusion.4
  251.4 1.8 collective-permute-start.3
  253.2 0.6 collective-permute-start.2
  253.8 1.0 collective-permute-start.1
  254.9 14.2 %shard_map.113 = bf16[3072,3072]{1,0:T(8,128)(2,1)} custom-call(bf16[512,3072]{1,0:T(8,128)(2,1)S(1)} %copy-done.7, bf16[512,3072]{1,0:T(8,128)(2,1)S(1)} %bitcast.29), custom_call_target="tpu_custom_call" | custom-call | flops 9663676416 | bytes 25165824 | tf_op jit(solution)/shard_map/pallas_call | solution.py:415
  269.1 1.2 convert_reduce_fusion
  270.3 2.9 %collective-permute-done.2 = bf16[64,3072]{1,0:T(8,128)(2,1)} collective-permute-done((bf16[64,3072]{1,0:T(8,128)(2,1)}, bf16[64,3072]{1,0:T(8,128)(2,1)}, u32[]{:S(2)}, u32[]{:S(2)}) %collective-permute-start.2) | collective-permute-done | bytes 393248 | tf_op jit(solution)/shard_map/ppermute | solution.py:445
  273.2 2.4 fusion.3
  275.6 0.6 copy.15
  (20 shorter events, 0.0 us)
Async XLA Ops:
  4.9 1.0 copy-start.2
  5.9 1.0 copy-start.3
  48.7 1.7 copy-start
  50.4 1.7 copy-start.4
  52.1 1.7 copy-start.6
  227.0 3.5 %copy-start.5 = (bf16[8,64,3072]{2,1,0:T(8,128)(2,1)S(1)}, bf16[8,64,3072]{2,1,0:T(8,128)(2,1)}, u32[]{:S(2)}) copy-start(bf16[8,64,3072]{2,1,0:T(8,128)(2,1)} %copy-done.4) | copy-start | bytes 9437188
  230.5 16.2 %collective-permute-start = (bf16[4,64,3072]{2,1,0:T(8,128)(2,1)}, bf16[4,64,3072]{2,1,0:T(8,128)(2,1)}, u32[]{:S(2)}, u32[]{:S(2)}) collective-permute-start(bf16[4,64,3072]{2,1,0:T(8,128)(2,1)} %fusion), channel_id=1, source_target_pairs={{0,4},{4,0},{8,12},{12,8},{16,20},{20,16},{24,28},{28,24},{1,5},{5... | collective-permute-start | bytes 4718600 | tf_op jit(solution)/shard_map/ppermute | solution.py:440
  230.5 1.9 copy-start.8
  232.4 14.3 %copy-start.10 = (f32[512,3072]{1,0:T(8,128)S(1)}, f32[512,3072]{1,0:T(8,128)}, u32[]{:S(2)}) copy-start(f32[512,3072]{1,0:T(8,128)} %get-tuple-element.15) | copy-start | bytes 18874372
  246.7 8.2 %copy-start.1 = (bf16[8,64,3072]{2,1,0:T(8,128)(2,1)S(1)}, bf16[8,64,3072]{2,1,0:T(8,128)(2,1)}, u32[]{:S(2)}) copy-start(bf16[8,64,3072]{2,1,0:T(8,128)(2,1)} %copy-done) | copy-start | bytes 9437188
  246.7 8.2 %copy-start.7 = (bf16[512,3072]{1,0:T(8,128)(2,1)S(1)}, bf16[512,3072]{1,0:T(8,128)(2,1)}, u32[]{:S(2)}) copy-start(bf16[512,3072]{1,0:T(8,128)(2,1)} %get-tuple-element.17.left) | copy-start | bytes 9437188
  248.7 1.7 copy-start.9
  251.4 19.0 %collective-permute-start.3 = (bf16[64,3072]{1,0:T(8,128)(2,1)}, bf16[64,3072]{1,0:T(8,128)(2,1)}, u32[]{:S(2)}, u32[]{:S(2)}) collective-permute-start(bf16[64,3072]{1,0:T(8,128)(2,1)} %get-tuple-element.20), channel_id=1, source_target_pairs={{0,24},{4,28},{8,0},{12,4},{16,8},{20,12},{24,16},{28,20},{1,25},{... | collective-permute-start | bytes 1179656 | tf_op jit(solution)/shard_map/ppermute | solution.py:445
  253.2 20.0 %collective-permute-start.2 = (bf16[64,3072]{1,0:T(8,128)(2,1)}, bf16[64,3072]{1,0:T(8,128)(2,1)}, u32[]{:S(2)}, u32[]{:S(2)}) collective-permute-start(bf16[64,3072]{1,0:T(8,128)(2,1)} %get-tuple-element.21), channel_id=1, source_target_pairs={{0,16},{4,20},{8,24},{12,28},{16,0},{20,4},{24,8},{28,12},{1,17},{... | collective-permute-start | bytes 1179656 | tf_op jit(solution)/shard_map/ppermute | solution.py:445
  253.8 19.4 %collective-permute-start.1 = (bf16[64,3072]{1,0:T(8,128)(2,1)S(1)}, bf16[64,3072]{1,0:T(8,128)(2,1)}, u32[]{:S(2)}, u32[]{:S(2)}) collective-permute-start(bf16[64,3072]{1,0:T(8,128)(2,1)S(1)} %get-tuple-element.19), channel_id=1, source_target_pairs={{0,8},{4,12},{8,16},{12,20},{16,24},{20,28},{24,0},{28,4},{1,9},{5... | collective-permute-start | bytes 1179656 | tf_op jit(solution)/shard_map/ppermute | solution.py:445
  269.1 6.5 %copy-start.11 = (f32[12,1,256]{2,1,0:T(1,128)S(1)}, f32[12,1,256]{2,1,0:T(1,128)}, u32[]{:S(2)}) copy-start(f32[12,1,256]{2,1,0:T(1,128)} %get-tuple-element.18) | copy-start | bytes 36868
